TPU v7x, 32 devices: a whole 2x2x4 slice. The times are simulated.
32 devices in a mesh: ctx: 4 (over y, x), dp: 8 (over z, core).
Axes of the slice: x: 2, y: 2, z: 4, core: 2. Of those that a mesh axis runs over, the one named last changes fastest.
Arguments:
- queries: bfloat16 [8, 512, 2048], P('dp', 'ctx'), may hold values from -8 to 8
- key_rows: bfloat16 [8, 512, 256], P('dp', 'ctx'), may hold values from -8 to 8
- value_rows: bfloat16 [8, 512, 256], P('dp', 'ctx'), may hold values from -6 to 6
- stream: bfloat16 [8, 512, 2048], P('dp', 'ctx'), may hold values from -6 to 6
- norm_gain: float32 [2048], replicated, may hold values from 0.1 to 1.9
- expert_ids: int32 [8, 512, 8], P('dp', 'ctx'), may hold values from 0 to 127, all different within a row; in each aligned block of 128 rows (0 to 127, 128 to 255, ..., all dimensions but the last counted through in order) at most 12 rows name the same one
- gate_values: float32 [8, 512, 8], P('dp', 'ctx'), may hold values from 0.1 to 1
- w_gate: bfloat16 [8, 2048, 384], P('dp', 'ctx'), may hold values from -0.125 to 0.125
- w_up: bfloat16 [8, 2048, 384], P('dp', 'ctx'), may hold values from -0.125 to 0.125
- w_down: bfloat16 [8, 384, 2048], P('dp', None, 'ctx'), may hold values from -0.3125 to 0.3125
Outputs:
- attended: bfloat16 [8, 512, 2048], P('dp', 'ctx')
- expert_out: bfloat16 [8, 512, 2048], P('dp', 'ctx')
Inputs may be any that keep to these rules, and one draw needn't show every extreme that they name: `expert_ids`: among the rows of one device, no expert is chosen by more than 12 rows; some expert reaches 12.
All inputs are finite; a program needn't handle non-finite values.
Results may differ from a plain program's by a relative error of at most 0.012.
Values may be sent and summed in bfloat16 or wider, within the bound.
A program may use at most 64 MiB of HBM per device.

v0:
```python
import math

import jax
import jax.numpy as jnp
from jax import lax
from jax.sharding import PartitionSpec as P

HD = 128
CAP = 12


masked_score = -1e30


def passed_along(block, axis, distance):
    devices = range(lax.axis_size(axis))
    route = [(i - distance, i) for i in devices if i - distance in devices]
    return lax.ppermute(block, axis, route)


def attend_block(state, query_blocks, key_block, value_block, query_pos, key_start):
    largest, total, accum = state
    scale = 1.0 / math.sqrt(query_blocks.shape[-1])
    scores = (
        jnp.einsum("hrd,hkd->hrk", query_blocks, key_block, preferred_element_type=jnp.float32)
        * scale
    )
    key_pos = key_start + jnp.arange(key_block.shape[1], dtype=jnp.int32)
    allowed = key_pos[None, None, :] <= query_pos[None, :, None]
    block_max = jnp.max(jnp.where(allowed, scores, masked_score), axis=-1)
    new_max = jnp.maximum(largest, block_max)
    weights = jnp.where(allowed, jnp.exp(scores - new_max[..., None]), 0.0)
    rescale = jnp.exp(largest - new_max)
    total = total * rescale + jnp.sum(weights, axis=-1)
    accum = accum * rescale[..., None] + jnp.einsum(
        "hrk,hkd->hrd",
        weights.astype(jnp.bfloat16),
        value_block,
        preferred_element_type=jnp.float32,
    )
    return (new_max, total, accum)


def shards(
    queries, key_rows, value_rows, stream, norm_gain, expert_ids, gate_values, w_gate, w_up, w_down
):
    tokens = queries.shape[1]
    heads_kv = key_rows.shape[2] // HD
    group = queries.shape[2] // key_rows.shape[2]
    query_blocks = (
        queries[0]
        .reshape(tokens, heads_kv, group, HD)
        .transpose(1, 2, 0, 3)
        .reshape(heads_kv, group * tokens, HD)
    )
    key_local = key_rows[0].reshape(tokens, heads_kv, HD).transpose(1, 0, 2)
    value_local = value_rows[0].reshape(tokens, heads_kv, HD).transpose(1, 0, 2)
    block_pos = lax.axis_index("ctx")
    block_count = lax.axis_size("ctx")
    query_pos = block_pos * tokens + jnp.arange(group * tokens, dtype=jnp.int32) % tokens
    last_query = block_pos * tokens + tokens - 1
    state = (
        jnp.full((heads_kv, group * tokens), masked_score, jnp.float32),
        jnp.zeros((heads_kv, group * tokens), jnp.float32),
        jnp.zeros((heads_kv, group * tokens, HD), jnp.float32),
    )

    def maybe_attend(current, key_block, value_block, key_start):

        def compute(inner):
            return attend_block(inner, query_blocks, key_block, value_block, query_pos, key_start)

        def unchanged(inner):
            return inner

        return lax.cond(key_start <= last_query, compute, unchanged, current)

    state = attend_block(state, query_blocks, key_local, value_local, query_pos, block_pos * tokens)

    def pass_turn(turn, carry):
        current, key_block, value_block = carry
        key_block, value_block = passed_along((key_block, value_block), "ctx", 1)
        source = (block_pos - turn - 1) % block_count
        current = maybe_attend(current, key_block, value_block, source * tokens)
        return (current, key_block, value_block)

    state, key_last, value_last = lax.fori_loop(
        0, block_count - 1, pass_turn, (state, key_local, value_local)
    )
    largest, total, accum = state
    attended = (accum / total[..., None]).reshape(heads_kv, group, tokens, HD).transpose(2, 0, 1, 3)
    attended = attended.reshape(1, tokens, heads_kv * group * HD).astype(jnp.bfloat16)
    width = stream.shape[2]
    rows_in = stream[0].astype(jnp.float32)
    normed = (
        rows_in * lax.rsqrt(jnp.mean(rows_in * rows_in, axis=-1, keepdims=True) + 1e-06) * norm_gain
    ).astype(jnp.bfloat16)
    owners = lax.axis_size("dp")
    slots = owners * CAP
    top_count = expert_ids.shape[2]
    chosen = expert_ids[0].reshape(-1)
    weights_flat = gate_values[0].reshape(-1)
    owner_hot = (chosen[:, None] == jnp.arange(owners, dtype=jnp.int32)[None, :]).astype(jnp.int32)
    ranks = jnp.sum((jnp.cumsum(owner_hot, axis=0) - 1) * owner_hot, axis=1)
    target = jnp.where(chosen < owners, chosen * CAP + ranks, -1)
    slot_hot = target[:, None] == jnp.arange(slots, dtype=jnp.int32)[None, :]
    placement = jnp.sum(
        slot_hot.astype(jnp.float32).reshape(tokens, top_count, slots), axis=1
    ).astype(jnp.bfloat16)
    slot_weight = jnp.sum(jnp.where(slot_hot, weights_flat[:, None], 0.0), axis=0)
    outgoing = jnp.einsum(
        "ts,td->sd", placement, normed, preferred_element_type=jnp.float32
    ).astype(jnp.bfloat16)
    arrived = lax.all_to_all(
        outgoing.reshape(owners, CAP, width), "dp", split_axis=0, concat_axis=0, tiled=True
    ).reshape(slots, width)
    gate_piece = lax.all_gather(w_gate, "ctx", axis=1, tiled=True)
    up_piece = lax.all_gather(w_up, "ctx", axis=1, tiled=True)
    gate_sum = jnp.dot(arrived, gate_piece[0], preferred_element_type=jnp.float32)
    up_sum = jnp.dot(arrived, up_piece[0], preferred_element_type=jnp.float32)
    hidden = (jax.nn.silu(gate_sum) * up_sum).astype(jnp.bfloat16)
    produced = jnp.dot(
        hidden,
        lax.all_gather(w_down, "ctx", axis=2, tiled=True)[0],
        preferred_element_type=jnp.float32,
    )
    answers = produced.astype(jnp.bfloat16).reshape(owners, CAP, width)
    returned = lax.all_to_all(answers, "dp", split_axis=0, concat_axis=0, tiled=True).reshape(
        slots, width
    )
    weighted = returned.astype(jnp.float32) * slot_weight[:, None]
    upper_part = weighted.astype(jnp.bfloat16)
    lower_part = (weighted - upper_part.astype(jnp.float32)).astype(jnp.bfloat16)
    mixed = jnp.dot(placement, upper_part, preferred_element_type=jnp.float32) + jnp.dot(
        placement, lower_part, preferred_element_type=jnp.float32
    )
    expert_out = mixed.astype(jnp.bfloat16).reshape(1, tokens, width)
    return (attended, expert_out)


def solution(mesh):
    placed = (
        P("dp", "ctx", None),
        P("dp", "ctx", None),
        P("dp", "ctx", None),
        P("dp", "ctx", None),
        P(),
        P("dp", "ctx", None),
        P("dp", "ctx", None),
        P("dp", "ctx", None),
        P("dp", "ctx", None),
        P("dp", None, "ctx"),
    )
    return jax.shard_map(
        shards,
        mesh=mesh,
        in_specs=placed,
        out_specs=(P("dp", "ctx", None), P("dp", "ctx", None)),
        check_vma=False,
    )
```

profile of v0, /device:TPU:0, one launch (start us, length us, event | category | flops | bytes accessed | tf_op | source)
XLA Modules:
  0.0 157.9 jit_solution(8161995407081077352)
XLA Ops:
  7.2 0.7 all-gather.4.cloned.1.call-update
  8.0 0.7 all-gather.6.cloned.1.call-update
  8.7 0.7 all-gather.8.cloned.1.call-update
  9.4 0.8 copy.42
  10.2 0.1 eq.59
  10.4 2.3 %reduce-window.6 = s32[8,8,128]{2,1,0:T(8,128)S(1)} reduce-window(s32[8,8,128]{2,1,0:T(8,128)S(1)} %fusion.50, s32[]{:T(128)} %constant.106.clone.1), window={size=1x1x128 pad=0_0x0_0x127_0}, to_apply=%region_8.9 | reduce-window | flops 1040384 | bytes 65540 | tf_op jit(solution)/shard_map/reduce-window
  12.7 0.3 slice_reduce_fusion
  12.9 0.2 reduce-window.9
  13.5 0.2 fusion.25
  13.7 0.4 convolution_convert_fusion.1
  14.1 0.9 reshape.192
  14.9 6.5 %all-to-all-start = ((bf16[8,12,2048]{2,1,0:T(8,128)(2,1)}), bf16[8,12,2048]{2,1,0:T(8,128)(2,1)S(1)}, u32[]{:S(2)}, u32[]{:S(2)}) async-start(bf16[8,12,2048]{2,1,0:T(8,128)(2,1)} %reshape.192), calls=%async_computation | async-start | bytes 1048576 | tf_op jit(solution)/shard_map/all_to_all | solution.py:114
  21.4 0.1 copy.52
  21.6 0.1 copy.33
  21.7 0.1 copy.34
  21.8 0.1 broadcast_compare_fusion.1
  22.0 0.4 select_reduce_fusion.1
  22.4 0.1 copy.39
  22.6 0.1 copy.47
  22.7 0.1 broadcast_in_dim.81
  22.8 0.1 copy.36
  22.9 0.1 copy.40
  23.0 0.2 fusion.29
  23.3 0.8 convolution_add_fusion.2
  24.1 12.7 %all-to-all-done = bf16[8,12,2048]{2,1,0:T(8,128)(2,1)S(1)} async-done(((bf16[8,12,2048]{2,1,0:T(8,128)(2,1)}), bf16[8,12,2048]{2,1,0:T(8,128)(2,1)S(1)}, u32[]{:S(2)}, u32[]{:S(2)}) %all-to-all-start) | async-done | bytes 393248 | tf_op jit(solution)/shard_map/all_to_all | solution.py:114
  36.9 6.7 %all-gather.4.cloned.1.call-done = bf16[1,2048,384]{2,1,0:T(8,128)(2,1)} async-done(((bf16[1,512,384]{2,1,0:T(8,128)(2,1)}), bf16[1,2048,384]{2,1,0:T(8,128)(2,1)}) %all-gather.4.cloned.1.call-update) | async-done | bytes 1572880 | tf_op jit(solution)/shard_map/all_gather | solution.py:117
  43.6 1.8 %fusion.15 = f32[96,384]{1,0:T(8,128)S(1)} fusion(bf16[96,2048]{1,0:T(8,128)(2,1)S(1)} %reshape.193, bf16[1,2048,384]{2,1,0:T(8,128)(2,1)} %all-gather.4.cloned.1.call-done), kind=kOutput, calls=%fused_computation.27 | convolution fusion | flops 150994944 | bytes 2113536 | tf_op jit(solution)/shard_map/dot_general | solution.py:119
  45.4 31.0 %all-gather.6.cloned.1.call-done = bf16[1,2048,384]{2,1,0:T(8,128)(2,1)} async-done(((bf16[1,512,384]{2,1,0:T(8,128)(2,1)}), bf16[1,2048,384]{2,1,0:T(8,128)(2,1)}) %all-gather.6.cloned.1.call-update) | async-done | bytes 1572880 | tf_op jit(solution)/shard_map/all_gather | solution.py:118
  76.4 32.7 %all-gather.8.cloned.1.call-done = bf16[1,384,2048]{2,1,0:T(8,128)(2,1)} async-done(((bf16[1,384,512]{2,1,0:T(8,128)(2,1)}), bf16[1,384,2048]{2,1,0:T(8,128)(2,1)}) %all-gather.8.cloned.1.call-update) | async-done | bytes 1572880 | tf_op jit(solution)/shard_map/all_gather | solution.py:124
  109.1 2.7 %convolution_convert_fusion = bf16[96,2048]{1,0:T(8,128)(2,1)S(1)} fusion(bf16[1,384,2048]{2,1,0:T(8,128)(2,1)} %all-gather.8.cloned.1.call-done, bf16[96,2048]{1,0:T(8,128)(2,1)S(1)} %reshape.193, bf16[1,2048,384]{2,1,0:T(8,128)(2,1)} %all-gather.6.cloned.1.call-done, f32[96,384]{1,0:T(8,128)S(1)} %fusion.15), kind=kOutput, calls=%fused_computation.21 | convolution fusion | flops 302407680 | bytes 4079616 | tf_op jit(solution)/shard_map/dot_general | solution.py:122
  111.8 0.9 reshape.194
  112.7 4.6 %all-to-all-start.1 = ((bf16[8,12,2048]{2,1,0:T(8,128)(2,1)}), bf16[8,12,2048]{2,1,0:T(8,128)(2,1)S(1)}, u32[]{:S(2)}, u32[]{:S(2)}) async-start(bf16[8,12,2048]{2,1,0:T(8,128)(2,1)} %reshape.194), calls=%async_computation.1 | async-start | bytes 1048576 | tf_op jit(solution)/shard_map/all_to_all | solution.py:128
  117.3 30.6 %while.24 = (s32[]{:T(128)}, f32[2,1024]{1,0:T(2,128)S(1)}, f32[2,1024]{1,0:T(2,128)S(1)}, f32[2,1024,128]{2,1,0:T(8,128)S(1)}, bf16[2,128,128]{2,1,0:T(8,128)(2...) while((s32[]{:T(128)}, f32[2,1024]{1,0:T(2,128)S(1)}, ...), condition=%wide.region_7.8_spmd.clone, body=%wide.region_2.7_spmd.clone.sunk | while | flops 137243792 | bytes 7378492 | solution.py:87
  117.3 3.3 %collective-permute-start = (bf16[2,128,128]{2,1,0:T(8,128)(2,1)S(1)}, bf16[2,128,128]{2,1,0:T(8,128)(2,1)S(1)}, u32[]{:S(2)}, u32[]{:S(2)}) collective-permute-start(bf16[2,128,128]{2,1,0:T(8,128)(2,1)S(1)} %get-tuple-element.508), channel_id=1, source_target_pairs={{0,8},{8,16},{16,24},{1,9},{9,17},{17,25},{2,10},{10,18},{18,26},{... | collective-permute-start | bytes 196616 | tf_op jit(solution)/shard_map/while/body/eval_jaxpr/ppermute | solution.py:18
  120.7 3.4 %collective-permute-start.1 = (bf16[2,128,128]{2,1,0:T(8,128)(2,1)S(1)}, bf16[2,128,128]{2,1,0:T(8,128)(2,1)S(1)}, u32[]{:S(2)}, u32[]{:S(2)}) collective-permute-start(bf16[2,128,128]{2,1,0:T(8,128)(2,1)S(1)} %get-tuple-element.509), channel_id=1, source_target_pairs={{0,8},{8,16},{16,24},{1,9},{9,17},{17,25},{2,10},{10,18},{18,26},{... | collective-permute-start | bytes 196616 | tf_op jit(solution)/shard_map/while/body/eval_jaxpr/ppermute | solution.py:18
  124.1 1.8 %collective-permute-done.1 = bf16[2,128,128]{2,1,0:T(8,128)(2,1)S(1)} collective-permute-done((bf16[2,128,128]{2,1,0:T(8,128)(2,1)S(1)}, bf16[2,128,128]{2,1,0:T(8,128)(2,1)S(1)}, u32[]{:S(2)}, u32[]{:S(2)}) %collective-permute-start.1) | collective-permute-done | bytes 65568 | tf_op jit(solution)/shard_map/while/body/eval_jaxpr/ppermute | solution.py:18
  126.0 5.9 %collective-permute-start = (bf16[2,128,128]{2,1,0:T(8,128)(2,1)S(1)}, bf16[2,128,128]{2,1,0:T(8,128)(2,1)S(1)}, u32[]{:S(2)}, u32[]{:S(2)}) collective-permute-start(bf16[2,128,128]{2,1,0:T(8,128)(2,1)S(1)} %get-tuple-element.508), channel_id=1, source_target_pairs={{0,8},{8,16},{16,24},{1,9},{9,17},{17,25},{2,10},{10,18},{18,26},{... | collective-permute-start | bytes 196616 | tf_op jit(solution)/shard_map/while/body/eval_jaxpr/ppermute | solution.py:18
  131.9 3.3 %collective-permute-start.1 = (bf16[2,128,128]{2,1,0:T(8,128)(2,1)S(1)}, bf16[2,128,128]{2,1,0:T(8,128)(2,1)S(1)}, u32[]{:S(2)}, u32[]{:S(2)}) collective-permute-start(bf16[2,128,128]{2,1,0:T(8,128)(2,1)S(1)} %get-tuple-element.509), channel_id=1, source_target_pairs={{0,8},{8,16},{16,24},{1,9},{9,17},{17,25},{2,10},{10,18},{18,26},{... | collective-permute-start | bytes 196616 | tf_op jit(solution)/shard_map/while/body/eval_jaxpr/ppermute | solution.py:18
  135.3 1.8 %collective-permute-done.1 = bf16[2,128,128]{2,1,0:T(8,128)(2,1)S(1)} collective-permute-done((bf16[2,128,128]{2,1,0:T(8,128)(2,1)S(1)}, bf16[2,128,128]{2,1,0:T(8,128)(2,1)S(1)}, u32[]{:S(2)}, u32[]{:S(2)}) %collective-permute-start.1) | collective-permute-done | bytes 65568 | tf_op jit(solution)/shard_map/while/body/eval_jaxpr/ppermute | solution.py:18
  137.2 4.3 %collective-permute-start = (bf16[2,128,128]{2,1,0:T(8,128)(2,1)S(1)}, bf16[2,128,128]{2,1,0:T(8,128)(2,1)S(1)}, u32[]{:S(2)}, u32[]{:S(2)}) collective-permute-start(bf16[2,128,128]{2,1,0:T(8,128)(2,1)S(1)} %get-tuple-element.508), channel_id=1, source_target_pairs={{0,8},{8,16},{16,24},{1,9},{9,17},{17,25},{2,10},{10,18},{18,26},{... | collective-permute-start | bytes 196616 | tf_op jit(solution)/shard_map/while/body/eval_jaxpr/ppermute | solution.py:18
  141.5 4.5 %collective-permute-start.1 = (bf16[2,128,128]{2,1,0:T(8,128)(2,1)S(1)}, bf16[2,128,128]{2,1,0:T(8,128)(2,1)S(1)}, u32[]{:S(2)}, u32[]{:S(2)}) collective-permute-start(bf16[2,128,128]{2,1,0:T(8,128)(2,1)S(1)} %get-tuple-element.509), channel_id=1, source_target_pairs={{0,8},{8,16},{16,24},{1,9},{9,17},{17,25},{2,10},{10,18},{18,26},{... | collective-permute-start | bytes 196616 | tf_op jit(solution)/shard_map/while/body/eval_jaxpr/ppermute | solution.py:18
  146.0 1.8 %collective-permute-done.1 = bf16[2,128,128]{2,1,0:T(8,128)(2,1)S(1)} collective-permute-done((bf16[2,128,128]{2,1,0:T(8,128)(2,1)S(1)}, bf16[2,128,128]{2,1,0:T(8,128)(2,1)S(1)}, u32[]{:S(2)}, u32[]{:S(2)}) %collective-permute-start.1) | collective-permute-done | bytes 65568 | tf_op jit(solution)/shard_map/while/body/eval_jaxpr/ppermute | solution.py:18
  147.9 0.3 divide_convert_fusion
  148.2 0.3 copy.56
  148.6 1.0 convert_element_type.88
  149.6 0.1 select_reduce_fusion.2
  149.8 0.4 fusion.30
  150.2 1.2 fusion.11
  (50 shorter events, 0.8 us)
Async XLA Ops:
  7.2 6.3 %copy-start = (bf16[1,128,2048]{2,1,0:T(8,128)(2,1)S(1)}, bf16[1,128,2048]{2,1,0:T(8,128)(2,1)}, u32[]{:S(2)}) copy-start(bf16[1,128,2048]{2,1,0:T(8,128)(2,1)} %param.17) | copy-start | bytes 1572868
  7.2 6.5 %copy-start.5 = (f32[2048]{0:T(1024)S(1)}, f32[2048]{0:T(1024)}, u32[]{:S(2)}) copy-start(f32[2048]{0:T(1024)} %param.18) | copy-start | bytes 24580
  7.2 36.4 %all-gather.4.cloned.1.call-start = ((), (), s32[]{:S(2)}) async-start(), calls=%async_computation.2 | async-start | bytes 1966080 | tf_op jit(solution)/shard_map/all_gather | solution.py:117
  7.9 68.5 %all-gather.6.cloned.1.call-start = ((), (), s32[]{:S(2)}) async-start(), calls=%async_computation.3 | async-start | bytes 1966080 | tf_op jit(solution)/shard_map/all_gather | solution.py:118
  8.7 100.4 %all-gather.8.cloned.1.call-start = ((), (), s32[]{:S(2)}) async-start(), calls=%async_computation.4 | async-start | bytes 1966080 | tf_op jit(solution)/shard_map/all_gather | solution.py:124
  13.6 7.8 %copy-start.1 = (bf16[1,128,2048]{2,1,0:T(8,128)(2,1)S(1)}, bf16[1,128,2048]{2,1,0:T(8,128)(2,1)}, u32[]{:S(2)}) copy-start(bf16[1,128,2048]{2,1,0:T(8,128)(2,1)} %param.14) | copy-start | bytes 1572868
  14.9 6.8 %copy-start.2 = (bf16[1,128,256]{2,1,0:T(8,128)(2,1)S(1)}, bf16[1,128,256]{2,1,0:T(8,128)(2,1)}, u32[]{:S(2)}) copy-start(bf16[1,128,256]{2,1,0:T(8,128)(2,1)} %param.15) | copy-start | bytes 196612
  14.9 21.8 %all-to-all-start = ((bf16[8,12,2048]{2,1,0:T(8,128)(2,1)}), bf16[8,12,2048]{2,1,0:T(8,128)(2,1)S(1)}, u32[]{:S(2)}, u32[]{:S(2)}) async-start(bf16[8,12,2048]{2,1,0:T(8,128)(2,1)} %reshape.192), calls=%async_computation | async-start | bytes 1048576 | tf_op jit(solution)/shard_map/all_to_all | solution.py:114
  21.5 1.0 copy-start.4
  21.5 1.2 copy-start.3
  112.7 37.0 %all-to-all-start.1 = ((bf16[8,12,2048]{2,1,0:T(8,128)(2,1)}), bf16[8,12,2048]{2,1,0:T(8,128)(2,1)S(1)}, u32[]{:S(2)}, u32[]{:S(2)}) async-start(bf16[8,12,2048]{2,1,0:T(8,128)(2,1)} %reshape.194), calls=%async_computation.1 | async-start | bytes 1048576 | tf_op jit(solution)/shard_map/all_to_all | solution.py:128
  117.3 6.8 %collective-permute-start = (bf16[2,128,128]{2,1,0:T(8,128)(2,1)S(1)}, bf16[2,128,128]{2,1,0:T(8,128)(2,1)S(1)}, u32[]{:S(2)}, u32[]{:S(2)}) collective-permute-start(bf16[2,128,128]{2,1,0:T(8,128)(2,1)S(1)} %get-tuple-element.508), channel_id=1, source_target_pairs={{0,8},{8,16},{16,24},{1,9},{9,17},{17,25},{2,10},{10,18},{18,26},{... | collective-permute-start | bytes 196616 | tf_op jit(solution)/shard_map/while/body/eval_jaxpr/ppermute | solution.py:18
  120.7 5.3 %collective-permute-start.1 = (bf16[2,128,128]{2,1,0:T(8,128)(2,1)S(1)}, bf16[2,128,128]{2,1,0:T(8,128)(2,1)S(1)}, u32[]{:S(2)}, u32[]{:S(2)}) collective-permute-start(bf16[2,128,128]{2,1,0:T(8,128)(2,1)S(1)} %get-tuple-element.509), channel_id=1, source_target_pairs={{0,8},{8,16},{16,24},{1,9},{9,17},{17,25},{2,10},{10,18},{18,26},{... | collective-permute-start | bytes 196616 | tf_op jit(solution)/shard_map/while/body/eval_jaxpr/ppermute | solution.py:18
  126.0 9.3 %collective-permute-start = (bf16[2,128,128]{2,1,0:T(8,128)(2,1)S(1)}, bf16[2,128,128]{2,1,0:T(8,128)(2,1)S(1)}, u32[]{:S(2)}, u32[]{:S(2)}) collective-permute-start(bf16[2,128,128]{2,1,0:T(8,128)(2,1)S(1)} %get-tuple-element.508), channel_id=1, source_target_pairs={{0,8},{8,16},{16,24},{1,9},{9,17},{17,25},{2,10},{10,18},{18,26},{... | collective-permute-start | bytes 196616 | tf_op jit(solution)/shard_map/while/body/eval_jaxpr/ppermute | solution.py:18
  131.9 5.2 %collective-permute-start.1 = (bf16[2,128,128]{2,1,0:T(8,128)(2,1)S(1)}, bf16[2,128,128]{2,1,0:T(8,128)(2,1)S(1)}, u32[]{:S(2)}, u32[]{:S(2)}) collective-permute-start(bf16[2,128,128]{2,1,0:T(8,128)(2,1)S(1)} %get-tuple-element.509), channel_id=1, source_target_pairs={{0,8},{8,16},{16,24},{1,9},{9,17},{17,25},{2,10},{10,18},{18,26},{... | collective-permute-start | bytes 196616 | tf_op jit(solution)/shard_map/while/body/eval_jaxpr/ppermute | solution.py:18
  137.2 8.8 %collective-permute-start = (bf16[2,128,128]{2,1,0:T(8,128)(2,1)S(1)}, bf16[2,128,128]{2,1,0:T(8,128)(2,1)S(1)}, u32[]{:S(2)}, u32[]{:S(2)}) collective-permute-start(bf16[2,128,128]{2,1,0:T(8,128)(2,1)S(1)} %get-tuple-element.508), channel_id=1, source_target_pairs={{0,8},{8,16},{16,24},{1,9},{9,17},{17,25},{2,10},{10,18},{18,26},{... | collective-permute-start | bytes 196616 | tf_op jit(solution)/shard_map/while/body/eval_jaxpr/ppermute | solution.py:18
  141.5 6.4 %collective-permute-start.1 = (bf16[2,128,128]{2,1,0:T(8,128)(2,1)S(1)}, bf16[2,128,128]{2,1,0:T(8,128)(2,1)S(1)}, u32[]{:S(2)}, u32[]{:S(2)}) collective-permute-start(bf16[2,128,128]{2,1,0:T(8,128)(2,1)S(1)} %get-tuple-element.509), channel_id=1, source_target_pairs={{0,8},{8,16},{16,24},{1,9},{9,17},{17,25},{2,10},{10,18},{18,26},{... | collective-permute-start | bytes 196616 | tf_op jit(solution)/shard_map/while/body/eval_jaxpr/ppermute | solution.py:18
Sparse Core Ops, SparseCore 0:
  9.9 33.6 all-gather.3
  45.4 30.9 all-gather.5
  78.2 30.8 all-gather.7
where the time goes:
time: 158 us
  waiting for transfers between devices  90.7 us (57%)
  starting transfers between devices  35.9 us (23%)
  between operations  14 us (9%)
  matrix products  7.62 us (5%)
  local copies, waits for them, and re-layouts  5.68 us (4%)
  other arithmetic  3.7 us (2%)
    all_gather x1, waiting for transfers between devices, shards(): lax.all_gather(w_down, 'ctx', axis=2, tiled=True)[0]  32.7 us
    all_gather x1, waiting for transfers between devices, shards(): up_piece = lax.all_gather(w_up, 'ctx', axis=1, tiled=True)  31 us
    ppermute x6, starting transfers between devices, passed_along(): return lax.ppermute(block, axis, route)  24.8 us
    all_to_all x1, waiting for transfers between devices, shards(): lax.all_to_all(outgoing.reshape(owners, CAP, width), 'dp', split_axis=0,...  12.7 us
    all_gather x1, waiting for transfers between devices, shards(): gate_piece = lax.all_gather(w_gate, 'ctx', axis=1, tiled=True)  6.71 us
    all_to_all x1, starting transfers between devices, shards(): lax.all_to_all(outgoing.reshape(owners, CAP, width), 'dp', split_axis=0,...  6.47 us
    ppermute x6, waiting for transfers between devices, passed_along(): return lax.ppermute(block, axis, route)  5.52 us
    all_to_all x1, starting transfers between devices, shards(): lax.all_to_all(answers, 'dp', split_axis=0, concat_axis=0, tiled=True)  4.59 us
  transfers between devices with their start and end apart: 11, of which 7 were waited for; matrix products, arithmetic and copies ran while one was open for 7% of the time, Pallas kernels for 0%

commit v1 on v0

v1 whole, which is shorter than its diff:
```python
import functools
import math

import jax
import jax.numpy as jnp
from jax import lax
from jax.experimental import pallas as pl
from jax.experimental.pallas import tpu as pltpu
from jax.sharding import PartitionSpec as P

HD = 128
SLOT = 16
MESH = pl.DeviceIdType.MESH
hidden_score = -1e30


def fused(
    n_ctx, n_dp, split,
    q_ref, k_ref, v_ref, s_ref, gain_ref, ids_ref, gv_ref, wg_ref, wu_ref, wd_ref,
    att_ref, out_ref,
    outgoing, arrived, kbuf, vbuf, rs_out, rs_in, own, hid, answers, ret, w_hi, w_lo,
    k_send, k_recv, v_send, v_recv, a_send, a_recv, p_send, p_recv, h_send, h_recv,
    r_send, r_recv,
):
    my_c = lax.axis_index("ctx")
    my_d = lax.axis_index("dp")
    me = my_c * n_dp + my_d
    total = n_ctx * n_dp
    tokens, width = s_ref.shape[1], s_ref.shape[2]
    slots = n_dp * SLOT
    col = width // n_ctx
    units = wg_ref.shape[2]
    heads = q_ref.shape[2] // HD
    kv_heads = k_ref.shape[2] // HD
    group = heads // kv_heads

    barrier = pltpu.get_barrier_semaphore()

    def greet(i, carry):
        peer = lax.rem(me + i, total)
        pl.semaphore_signal(
            barrier, inc=1, device_id=(peer // n_dp, lax.rem(peer, n_dp)), device_id_type=MESH
        )
        return carry

    lax.fori_loop(1, total, greet, 0)

    lane = lax.broadcasted_iota(jnp.int32, (tokens, slots), 1)
    expert = lane // SLOT
    hot = jnp.zeros((tokens, slots), jnp.float32)
    weight = jnp.zeros((tokens, slots), jnp.float32)
    ids = ids_ref[0]
    gates = gv_ref[0]
    for t in range(ids_ref.shape[2]):
        hit = ids[:, t : t + 1] == expert
        hot = hot + jnp.where(hit, 1.0, 0.0)
        weight = weight + jnp.where(hit, gates[:, t : t + 1], 0.0)
    rows_i = lax.broadcasted_iota(jnp.int32, (tokens, tokens), 0)
    cols_i = lax.broadcasted_iota(jnp.int32, (tokens, tokens), 1)
    before = jnp.where(cols_i < rows_i, 1.0, 0.0).astype(jnp.bfloat16)
    rank = jnp.dot(before, hot.astype(jnp.bfloat16), preferred_element_type=jnp.float32)
    place = jnp.where(rank == (lane % SLOT).astype(jnp.float32), hot, 0.0)
    weighted = place * weight
    upper = weighted.astype(jnp.bfloat16)
    w_hi[...] = upper
    w_lo[...] = (weighted - upper.astype(jnp.float32)).astype(jnp.bfloat16)
    select = place.T.astype(jnp.bfloat16)

    pl.semaphore_wait(barrier, total - 1)

    def ctx_copy(src, dst, send, recv, c):
        return pltpu.make_async_remote_copy(
            src_ref=src, dst_ref=dst, send_sem=send, recv_sem=recv,
            device_id=(c, my_d), device_id_type=MESH,
        )

    others = [lax.rem(my_c + i, n_ctx) for i in range(1, n_ctx)]
    for c in others:
        ctx_copy(k_ref.at[0], kbuf.at[my_c], k_send.at[c], k_recv.at[my_c], c).start()
        ctx_copy(v_ref.at[0], vbuf.at[my_c], v_send.at[c], v_recv.at[my_c], c).start()

    x = s_ref[0].astype(jnp.float32)
    normed = (
        x * lax.rsqrt(jnp.mean(x * x, axis=-1, keepdims=True) + 1e-06) * gain_ref[...]
    ).astype(jnp.bfloat16)
    for c in range(n_ctx):
        outgoing[c] = jnp.dot(
            select, normed[:, c * col : (c + 1) * col], preferred_element_type=jnp.float32
        ).astype(jnp.bfloat16)

    my_rows = pl.ds(pl.multiple_of(my_d * SLOT, SLOT), SLOT)

    def scatter(src, dst, send, recv, c, first):
        def one(i, carry):
            d = lax.rem(my_d + i, n_dp)
            pltpu.make_async_remote_copy(
                src_ref=src.at[c, pl.ds(pl.multiple_of(d * SLOT, SLOT), SLOT)],
                dst_ref=dst.at[my_c, my_rows],
                send_sem=send.at[c],
                recv_sem=recv.at[my_c],
                device_id=(c, d),
                device_id_type=MESH,
            ).start()
            return carry

        lax.fori_loop(first, n_dp, one, 0)

    def group_of(buf, send, recv, c, rows):
        part = buf.at[c, pl.ds(0, rows)]
        return pltpu.make_async_remote_copy(
            src_ref=part, dst_ref=part, send_sem=send.at[c], recv_sem=recv.at[c],
            device_id=(c, lax.rem(my_d + 1, n_dp)), device_id_type=MESH,
        )

    for c in others:
        scatter(outgoing, arrived, a_send, a_recv, c, 0)
    scatter(outgoing, arrived, a_send, a_recv, my_c, 1)
    arrived[my_c, my_rows] = outgoing[my_c, my_rows]
    kbuf[my_c] = k_ref[0]
    vbuf[my_c] = v_ref[0]
    for c in others:
        ctx_copy(k_ref.at[0], kbuf.at[c], k_send.at[c], k_recv.at[c], c).wait_recv()
        ctx_copy(v_ref.at[0], vbuf.at[c], v_send.at[c], v_recv.at[c], c).wait_recv()

    keys = n_ctx * tokens
    scale = 1.0 / math.sqrt(HD)

    def attend(first, last):
        def one(h, carry):
            at = pl.ds(pl.multiple_of(h * HD, HD), HD)
            kv_at = pl.ds(pl.multiple_of((h // group) * HD, HD), HD)
            k_all = kbuf[:, :, kv_at].reshape(keys, HD)
            v_all = vbuf[:, :, kv_at].reshape(keys, HD)
            scores = lax.dot_general(
                q_ref[0, :, at], k_all, (((1,), (1,)), ((), ())),
                preferred_element_type=jnp.float32,
            ) * scale
            q_pos = my_c * tokens + lax.broadcasted_iota(jnp.int32, (tokens, keys), 0)
            k_pos = lax.broadcasted_iota(jnp.int32, (tokens, keys), 1)
            scores = jnp.where(k_pos <= q_pos, scores, hidden_score)
            probs = jnp.exp(scores - jnp.max(scores, axis=-1, keepdims=True))
            mass = jnp.sum(probs, axis=-1, keepdims=True)
            mixed = jnp.dot(probs.astype(jnp.bfloat16), v_all, preferred_element_type=jnp.float32)
            att_ref[0, :, at] = (mixed / mass).astype(jnp.bfloat16)
            return carry

        lax.fori_loop(first, last, one, 0)

    marks = [0] + [heads * s // 16 for s in split] + [heads]
    attend(marks[0], marks[1])

    for c in others:
        group_of(arrived, a_send, a_recv, c, slots).wait_recv()
        rows = arrived[c]
        rs_out[c, :, :units] = jnp.dot(
            rows, wg_ref[0], preferred_element_type=jnp.float32
        ).astype(jnp.bfloat16)
        rs_out[c, :, units:] = jnp.dot(
            rows, wu_ref[0], preferred_element_type=jnp.float32
        ).astype(jnp.bfloat16)
        ctx_copy(rs_out.at[c], rs_in.at[my_c], p_send.at[c], p_recv.at[my_c], c).start()
    group_of(arrived, a_send, a_recv, my_c, slots - SLOT).wait_recv()
    rows = arrived[my_c]
    own[:, :units] = jnp.dot(rows, wg_ref[0], preferred_element_type=jnp.float32)
    own[:, units:] = jnp.dot(rows, wu_ref[0], preferred_element_type=jnp.float32)
    attend(marks[1], marks[2])
    for c in others:
        ctx_copy(rs_out.at[c], rs_in.at[c], p_send.at[c], p_recv.at[c], c).wait_recv()
    sums = own[...]
    for c in others:
        sums = sums + rs_in[c].astype(jnp.float32)
    gate = sums[:, :units]
    hid[my_c] = (gate / (1.0 + jnp.exp(-gate)) * sums[:, units:]).astype(jnp.bfloat16)
    for c in others:
        ctx_copy(hid.at[my_c], hid.at[my_c], h_send.at[c], h_recv.at[my_c], c).start()

    def answer(c):
        answers[c] = jnp.dot(hid[c], wd_ref[0], preferred_element_type=jnp.float32).astype(
            jnp.bfloat16
        )

    answer(my_c)
    scatter(answers, ret, r_send, r_recv, my_c, 1)
    ret[my_c, my_rows] = answers[my_c, my_rows]
    attend(marks[2], marks[3])
    for c in others:
        ctx_copy(hid.at[my_c], hid.at[c], h_send.at[c], h_recv.at[c], c).wait_recv()
        answer(c)
        scatter(answers, ret, r_send, r_recv, c, 0)
    attend(marks[3], marks[4])

    def combine(c):
        part = ret[c]
        mixed = jnp.dot(w_hi[...], part, preferred_element_type=jnp.float32) + jnp.dot(
            w_lo[...], part, preferred_element_type=jnp.float32
        )
        out_ref[0, :, pl.ds(pl.multiple_of(c * col, col), col)] = mixed.astype(jnp.bfloat16)

    group_of(ret, r_send, r_recv, my_c, slots - SLOT).wait_recv()
    combine(my_c)
    for c in others:
        group_of(ret, r_send, r_recv, c, slots).wait_recv()
        combine(c)

    group_of(outgoing, a_send, a_recv, my_c, slots - SLOT).wait_send()
    group_of(answers, r_send, r_recv, my_c, slots - SLOT).wait_send()
    for c in others:
        ctx_copy(k_ref.at[0], kbuf.at[c], k_send.at[c], k_recv.at[c], c).wait_send()
        ctx_copy(v_ref.at[0], vbuf.at[c], v_send.at[c], v_recv.at[c], c).wait_send()
        group_of(outgoing, a_send, a_recv, c, slots).wait_send()
        ctx_copy(rs_out.at[c], rs_in.at[c], p_send.at[c], p_recv.at[c], c).wait_send()
        ctx_copy(hid.at[my_c], hid.at[c], h_send.at[c], h_recv.at[c], c).wait_send()
        group_of(answers, r_send, r_recv, c, slots).wait_send()


def shards(n_ctx, n_dp, queries, key_rows, value_rows, stream, norm_gain, *rest):
    tokens, width = stream.shape[1:]
    kv = key_rows.shape[2]
    units = rest[2].shape[2]
    slots = n_dp * SLOT
    col = width // n_ctx
    bf16, f32 = jnp.bfloat16, jnp.float32
    scratch = [
        ((n_ctx, slots, col), bf16),
        ((n_ctx, slots, col), bf16),
        ((n_ctx, tokens, kv), bf16),
        ((n_ctx, tokens, kv), bf16),
        ((n_ctx, slots, 2 * units), bf16),
        ((n_ctx, slots, 2 * units), bf16),
        ((slots, 2 * units), f32),
        ((n_ctx, slots, units), bf16),
        ((n_ctx, slots, col), bf16),
        ((n_ctx, slots, col), bf16),
        ((tokens, slots), bf16),
        ((tokens, slots), bf16),
    ]
    need = sum(math.prod(s) * jnp.dtype(t).itemsize for s, t in scratch)
    vmem = pl.BlockSpec(memory_space=pltpu.VMEM)
    return pl.pallas_call(
        functools.partial(fused, n_ctx, n_dp, (8, 12, 14)),
        out_shape=(
            jax.ShapeDtypeStruct(queries.shape, bf16),
            jax.ShapeDtypeStruct(stream.shape, bf16),
        ),
        in_specs=[vmem] * 10,
        out_specs=(vmem, vmem),
        scratch_shapes=[pltpu.VMEM(s, t) for s, t in scratch]
        + [pltpu.SemaphoreType.DMA((n_ctx,))] * 12,
        compiler_params=pltpu.CompilerParams(
            collective_id=0, has_side_effects=True, vmem_limit_bytes=need + (16 << 20)
        ),
    )(queries, key_rows, value_rows, stream, norm_gain.reshape(1, width), *rest)


def solution(mesh):
    rows = P("dp", "ctx", None)
    return jax.shard_map(
        functools.partial(shards, mesh.shape["ctx"], mesh.shape["dp"]),
        mesh=mesh,
        in_specs=(rows,) * 4 + (P(),) + (rows,) * 4 + (P("dp", None, "ctx"),),
        out_specs=(rows, rows),
        check_vma=False,
    )
```

time: 158 us -> 59.1 us (0.37)
  waiting for transfers between devices: 90.7 us -> 0 us
  Pallas kernels: 0 us -> 49.7 us
  starting transfers between devices: 35.9 us -> 0 us
  between operations: 14 us -> 0.69 us
  matrix products: 7.62 us -> 0 us
  other arithmetic: 3.7 us -> 0 us
  local copies, waits for them, and re-layouts: 5.68 us -> 8.28 us
    all_gather x3 -> x0, waiting for transfers between devices: 70.4 us -> none  [the longest x1 32.7 us: shards(): lax.all_gather(w_down, 'ctx', axis=2, tiled=True)[0]]
    pallas_call x0 -> x1, Pallas kernels: none -> 49.7 us  [shards(): pl.pallas_call(functools.partial(fused, n_ctx, n_dp, (8, 12, 14)), out_sh...]
    ppermute x6 -> x0, starting transfers between devices: 24.8 us -> none  [passed_along(): return lax.ppermute(block, axis, route)]
    all_to_all x2 -> x0, waiting for transfers between devices: 12.7 us -> none  [the longest x1 12.7 us: shards(): lax.all_to_all(outgoing.reshape(owners, CAP, width), 'dp', split_axis=0,...]
    all_to_all x2 -> x0, starting transfers between devices: 11.1 us -> none  [the longest x1 6.47 us: shards(): lax.all_to_all(outgoing.reshape(owners, CAP, width), 'dp', split_axis=0,...]
    dot_general x7 -> x0, matrix products: 7.62 us -> none  [the longest x1 2.73 us: shards(): jnp.dot(hidden, lax.all_gather(w_down, 'ctx', axis=2, tiled=True)[0], pre...]
    unnamed x19 -> x20, local copies, waits for them, and re-layouts: 1.5 us -> 8.28 us
    ppermute x6 -> x0, waiting for transfers between devices: 5.52 us -> none  [passed_along(): return lax.ppermute(block, axis, route)]
  transfers between devices with their start and end apart: 11 -> 0, of which waited for: 7 -> 0; matrix products, arithmetic and copies ran while one was open for 7% -> 0% of each run, Pallas kernels for 0% -> 0%
where the time goes in v1:
time: 59.1 us; the launch traced here: 58.6 us
  Pallas kernels  49.7 us (84%)
  local copies, waits for them, and re-layouts  8.28 us (14%)
  between operations  0.69 us (1%)
    pallas_call x1, Pallas kernels, shards(): pl.pallas_call(functools.partial(fused, n_ctx, n_dp, (8, 12, 14)), out_sh...  49.7 us
    unnamed x20, local copies, waits for them, and re-layouts  8.28 us

profile of v1, /device:TPU:0, one launch (start us, length us, event | category | flops | bytes accessed | tf_op | source)
XLA Modules:
  0.0 58.6 jit_solution(2650387917911354895)
XLA Ops:
  0.6 0.0 copy-start.5
  0.6 0.0 copy-start.6
  0.7 0.8 %copy.12.ids_ref = s32[1,128,8]{2,1,0:T(8,128)S(1)} copy(s32[1,128,8]{1,2,0:T(8,128)} %param.15) | data formatting | bytes 8192 | tf_op args[5]
  1.5 0.0 copy-start.7
  1.5 0.8 %copy.13.gv_ref = f32[1,128,8]{2,1,0:T(8,128)S(1)} copy(f32[1,128,8]{1,2,0:T(8,128)} %param.16) | data formatting | bytes 8192 | tf_op args[6]
  2.3 0.0 copy-done.5
  2.3 0.0 copy-done.6
  2.3 0.0 copy-done.7
  2.3 0.0 copy-start
  2.3 1.0 %copy-done = bf16[1,128,2048]{2,1,0:T(8,128)(2,1)S(1)} copy-done((bf16[1,128,2048]{2,1,0:T(8,128)(2,1)S(1)}, bf16[1,128,2048]{2,1,0:T(8,128)(2,1)}, u32[]{:S(2)}) %copy-start) | copy-done | bytes 524312
  3.3 0.0 copy-start.1
  3.3 1.0 %copy-done.1 = bf16[1,128,2048]{2,1,0:T(8,128)(2,1)S(1)} copy-done((bf16[1,128,2048]{2,1,0:T(8,128)(2,1)S(1)}, bf16[1,128,2048]{2,1,0:T(8,128)(2,1)}, u32[]{:S(2)}) %copy-start.1) | copy-done | bytes 524312
  4.4 0.0 copy-start.2
  4.4 1.0 %copy-done.2 = bf16[1,512,384]{2,1,0:T(8,128)(2,1)S(1)} copy-done((bf16[1,512,384]{2,1,0:T(8,128)(2,1)S(1)}, bf16[1,512,384]{2,1,0:T(8,128)(2,1)}, u32[]{:S(2)}) %copy-start.2) | copy-done | bytes 393240
  5.4 0.0 copy-start.3
  5.4 1.0 %copy-done.3 = bf16[1,512,384]{2,1,0:T(8,128)(2,1)S(1)} copy-done((bf16[1,512,384]{2,1,0:T(8,128)(2,1)S(1)}, bf16[1,512,384]{2,1,0:T(8,128)(2,1)}, u32[]{:S(2)}) %copy-start.3) | copy-done | bytes 393240
  6.4 0.0 copy-start.4
  6.4 1.0 %copy-done.4 = bf16[1,384,512]{2,1,0:T(8,128)(2,1)S(1)} copy-done((bf16[1,384,512]{2,1,0:T(8,128)(2,1)S(1)}, bf16[1,384,512]{2,1,0:T(8,128)(2,1)}, u32[]{:S(2)}) %copy-start.4) | copy-done | bytes 393240
  7.4 49.7 %shard_map.113 = (bf16[1,128,2048]{2,1,0:T(8,128)(2,1)S(1)}, bf16[1,128,2048]{2,1,0:T(8,128)(2,1)S(1)}) custom-call(bf16[1,128,2048]{2,1,0:T(8,128)(2,1)S(1)} %copy-done, bf16[1,128,256]{2,1,0:T(8,128)(2,1)S(1)} %copy-done.5, bf16[1,128,256]{2,1,0:T(8,128)(2,1)S(1)} %copy-done.6, bf16[1,128,2048]{2,1,0:T(8,128)(2,1)S(1)} %copy-done.1, ...), custom_call_target="tpu_custom_call" | custom-call | tf_op jit(solution)/shard_map/pallas_call | solution.py:239
  57.1 0.8 %copy.16 = bf16[1,128,2048]{2,1,0:T(8,128)(2,1)} copy(bf16[1,128,2048]{2,1,0:T(8,128)(2,1)S(1)} %get-tuple-element.4) | data formatting | bytes 1048576
  57.9 0.8 %copy.17 = bf16[1,128,2048]{2,1,0:T(8,128)(2,1)} copy(bf16[1,128,2048]{2,1,0:T(8,128)(2,1)S(1)} %get-tuple-element.5) | data formatting | bytes 1048576
Async XLA Ops:
  0.6 1.6 %copy-start.5 = (bf16[1,128,256]{2,1,0:T(8,128)(2,1)S(1)}, bf16[1,128,256]{2,1,0:T(8,128)(2,1)}, u32[]{:S(2)}) copy-start(bf16[1,128,256]{2,1,0:T(8,128)(2,1)} %k_ref.1) | copy-start | bytes 196612
  0.6 1.6 %copy-start.6 = (bf16[1,128,256]{2,1,0:T(8,128)(2,1)S(1)}, bf16[1,128,256]{2,1,0:T(8,128)(2,1)}, u32[]{:S(2)}) copy-start(bf16[1,128,256]{2,1,0:T(8,128)(2,1)} %v_ref.1) | copy-start | bytes 196612
  1.5 0.8 %copy-start.7 = (f32[2048]{0:T(1024)S(1)}, f32[2048]{0:T(1024)}, u32[]{:S(2)}) copy-start(f32[2048]{0:T(1024)} %param.14) | copy-start | bytes 24580
  2.3 1.0 %copy-start = (bf16[1,128,2048]{2,1,0:T(8,128)(2,1)S(1)}, bf16[1,128,2048]{2,1,0:T(8,128)(2,1)}, u32[]{:S(2)}) copy-start(bf16[1,128,2048]{2,1,0:T(8,128)(2,1)} %q_ref.1) | copy-start | bytes 1572868
  3.3 1.0 %copy-start.1 = (bf16[1,128,2048]{2,1,0:T(8,128)(2,1)S(1)}, bf16[1,128,2048]{2,1,0:T(8,128)(2,1)}, u32[]{:S(2)}) copy-start(bf16[1,128,2048]{2,1,0:T(8,128)(2,1)} %s_ref.1) | copy-start | bytes 1572868
  4.4 1.0 %copy-start.2 = (bf16[1,512,384]{2,1,0:T(8,128)(2,1)S(1)}, bf16[1,512,384]{2,1,0:T(8,128)(2,1)}, u32[]{:S(2)}) copy-start(bf16[1,512,384]{2,1,0:T(8,128)(2,1)} %wg_ref.1) | copy-start | bytes 1179652
  5.4 1.0 %copy-start.3 = (bf16[1,512,384]{2,1,0:T(8,128)(2,1)S(1)}, bf16[1,512,384]{2,1,0:T(8,128)(2,1)}, u32[]{:S(2)}) copy-start(bf16[1,512,384]{2,1,0:T(8,128)(2,1)} %wu_ref.1) | copy-start | bytes 1179652
  6.4 1.0 %copy-start.4 = (bf16[1,384,512]{2,1,0:T(8,128)(2,1)S(1)}, bf16[1,384,512]{2,1,0:T(8,128)(2,1)}, u32[]{:S(2)}) copy-start(bf16[1,384,512]{2,1,0:T(8,128)(2,1)} %wd_ref.1) | copy-start | bytes 1179652

commit v2 on v1

v2 whole, which is shorter than its diff:
```python
import functools
import math

import jax
import jax.numpy as jnp
from jax import lax
from jax.experimental import pallas as pl
from jax.experimental.pallas import tpu as pltpu
from jax.sharding import PartitionSpec as P

HD = 128
CAP = 12
TILE = 16
LANES = 128
MESH = pl.DeviceIdType.MESH
hidden_score = -1e30


def message_form(col):
    chunks = col // LANES
    if chunks * CAP % TILE == 0:
        return CAP, chunks
    return TILE, 1


def fused(
    n_ctx, n_dp, split,
    q_hbm, k_hbm, v_hbm, s_hbm, gain_hbm, ids_hbm, gv_hbm, wg_hbm, wu_hbm, wd_hbm,
    att_ref, out_ref,
    q_ref, s_ref, gain_ref, ids_ref, gv_ref, wgu, wd_ref,
    outgoing, arrived, kbuf, vbuf, rs_out, rs_in, own, hid, answers, ret,
    w_hi, w_lo, sort, unsort,
    k_send, k_recv, v_send, v_recv, a_send, a_recv, p_send, p_recv, h_send, h_recv,
    r_send, r_recv, load_sem,
):
    my_c = lax.axis_index("ctx")
    my_d = lax.axis_index("dp")
    me = my_c * n_dp + my_d
    total = n_ctx * n_dp
    tokens, width = s_ref.shape
    col = width // n_ctx
    slot, chunks = message_form(col)
    message = slot * chunks
    wide = col // chunks
    rows_all = n_dp * slot
    lines = n_dp * message
    units = wd_ref.shape[0]
    heads = q_ref.shape[1] // HD
    kv_heads = kbuf.shape[2] // HD
    group = heads // kv_heads

    pairs = (
        (ids_hbm.at[0], ids_ref),
        (gv_hbm.at[0], gv_ref),
        (s_hbm.at[0], s_ref),
        (gain_hbm, gain_ref),
        (wg_hbm.at[0], wgu.at[:, pl.ds(0, units)]),
        (wu_hbm.at[0], wgu.at[:, pl.ds(units, units)]),
        (k_hbm.at[0], kbuf.at[my_c]),
        (v_hbm.at[0], vbuf.at[my_c]),
        (q_hbm.at[0], q_ref),
        (wd_hbm.at[0], wd_ref),
    )
    loads = [pltpu.make_async_copy(a, b, load_sem.at[i]) for i, (a, b) in enumerate(pairs)]
    for load in loads:
        load.start()

    barrier = pltpu.get_barrier_semaphore()

    def greet(i, carry):
        peer = lax.rem(me + i, total)
        pl.semaphore_signal(
            barrier, inc=1, device_id=(peer // n_dp, lax.rem(peer, n_dp)), device_id_type=MESH
        )
        return carry

    lax.fori_loop(1, total, greet, 0)

    def parts_of(line):
        rest = lax.rem(line, message)
        return lax.div(line, message), lax.div(rest, slot), lax.rem(rest, slot)

    expert, chunk, place_rank = parts_of(lax.broadcasted_iota(jnp.int32, (lines, 1), 0))
    _, chunk_lane, rank_lane = parts_of(lax.broadcasted_iota(jnp.int32, (1, lines), 1))
    expert_lane = lax.div(lax.broadcasted_iota(jnp.int32, (1, lines), 1), message)
    if chunks > 1:
        goes = chunk * rows_all + expert * slot + place_rank
        goes_lane = chunk_lane * rows_all + expert_lane * slot + rank_lane
        square = (lines, lines)
        unsort[...] = jnp.where(
            lax.broadcasted_iota(jnp.int32, square, 1) == goes, 1.0, 0.0
        ).astype(jnp.bfloat16)
        sort[...] = jnp.where(
            lax.broadcasted_iota(jnp.int32, square, 0) == goes_lane, 1.0, 0.0
        ).astype(jnp.bfloat16)
    loads[0].wait()
    loads[1].wait()
    hot = jnp.zeros((lines, tokens), jnp.float32)
    weight = jnp.zeros((lines, tokens), jnp.float32)
    for t in range(ids_ref.shape[0]):
        hit = ids_ref[t : t + 1, :] == expert
        hot = jnp.where(hit, 1.0, hot)
        weight = jnp.where(hit, gv_ref[t : t + 1, :], weight)
    rows_i = lax.broadcasted_iota(jnp.int32, (tokens, tokens), 0)
    cols_i = lax.broadcasted_iota(jnp.int32, (tokens, tokens), 1)
    before = jnp.where(rows_i < cols_i, 1.0, 0.0).astype(jnp.bfloat16)
    rank = jnp.dot(hot.astype(jnp.bfloat16), before, preferred_element_type=jnp.float32)
    place = jnp.where(rank == place_rank.astype(jnp.float32), hot, 0.0)
    select = jnp.concatenate(
        [jnp.where(chunk == j, place, 0.0).astype(jnp.bfloat16) for j in range(chunks)], axis=1
    )

    loads[2].wait()
    loads[3].wait()
    x = s_ref[...].astype(jnp.float32)
    normed = (
        x * lax.rsqrt(jnp.mean(x * x, axis=-1, keepdims=True) + 1e-06) * gain_ref[...]
    ).astype(jnp.bfloat16)
    for c in range(n_ctx):
        stacked = jnp.concatenate(
            [normed[:, c * col + j * wide : c * col + (j + 1) * wide] for j in range(chunks)], axis=0
        )
        outgoing[c] = jnp.dot(select, stacked, preferred_element_type=jnp.float32).astype(
            jnp.bfloat16
        )

    pl.semaphore_wait(barrier, total - 1)

    def ctx_copy(src, dst, send, recv, c):
        return pltpu.make_async_remote_copy(
            src_ref=src, dst_ref=dst, send_sem=send, recv_sem=recv,
            device_id=(c, my_d), device_id_type=MESH,
        )

    others = [lax.rem(my_c + i, n_ctx) for i in range(1, n_ctx)]
    my_rows = pl.ds(pl.multiple_of(my_d * message, message), message)

    def scatter(src, dst, send, recv, c, first):
        def one(i, carry):
            d = lax.rem(my_d + i, n_dp)
            pltpu.make_async_remote_copy(
                src_ref=src.at[c, pl.ds(pl.multiple_of(d * message, message), message)],
                dst_ref=dst.at[my_c, my_rows],
                send_sem=send.at[c],
                recv_sem=recv.at[my_c],
                device_id=(c, d),
                device_id_type=MESH,
            ).start()
            return carry

        lax.fori_loop(first, n_dp, one, 0)

    def group_of(buf, send, recv, c, rows):
        part = buf.at[c, pl.ds(0, rows)]
        return pltpu.make_async_remote_copy(
            src_ref=part, dst_ref=part, send_sem=send.at[c], recv_sem=recv.at[c],
            device_id=(c, lax.rem(my_d + 1, n_dp)), device_id_type=MESH,
        )

    for c in others:
        scatter(outgoing, arrived, a_send, a_recv, c, 0)
    scatter(outgoing, arrived, a_send, a_recv, my_c, 1)
    for c in others:
        ctx_copy(k_hbm.at[0], kbuf.at[my_c], k_send.at[c], k_recv.at[my_c], c).start()
        ctx_copy(v_hbm.at[0], vbuf.at[my_c], v_send.at[c], v_recv.at[my_c], c).start()
    arrived[my_c, my_rows] = outgoing[my_c, my_rows]

    back = (place * weight).T
    for j in range(chunks):
        of_chunk = jnp.where(chunk_lane == j, back, 0.0)
        upper = of_chunk.astype(jnp.bfloat16)
        w_hi[j * tokens : (j + 1) * tokens] = upper
        w_lo[j * tokens : (j + 1) * tokens] = (of_chunk - upper.astype(jnp.float32)).astype(
            jnp.bfloat16
        )

    keys = n_ctx * tokens
    scale = 1.0 / math.sqrt(HD)

    def attend(first, last):
        def one(h, carry):
            at = pl.ds(pl.multiple_of(h * HD, HD), HD)
            kv_at = pl.ds(pl.multiple_of((h // group) * HD, HD), HD)
            k_all = kbuf[:, :, kv_at].reshape(keys, HD)
            v_all = vbuf[:, :, kv_at].reshape(keys, HD)
            scores = lax.dot_general(
                q_ref[:, at], k_all, (((1,), (1,)), ((), ())),
                preferred_element_type=jnp.float32,
            ) * scale
            q_pos = my_c * tokens + lax.broadcasted_iota(jnp.int32, (tokens, keys), 0)
            k_pos = lax.broadcasted_iota(jnp.int32, (tokens, keys), 1)
            scores = jnp.where(k_pos <= q_pos, scores, hidden_score)
            probs = jnp.exp(scores - jnp.max(scores, axis=-1, keepdims=True))
            mass = jnp.sum(probs, axis=-1, keepdims=True)
            mixed = jnp.dot(probs.astype(jnp.bfloat16), v_all, preferred_element_type=jnp.float32)
            att_ref[0, :, at] = (mixed / mass).astype(jnp.bfloat16)
            return carry

        lax.fori_loop(first, last, one, 0)

    mark = heads * split // 16

    def partial(c):
        block = arrived[c]
        if chunks > 1:
            block = jnp.dot(sort[...], block, preferred_element_type=jnp.float32).astype(
                jnp.bfloat16
            )
            block = jnp.concatenate(
                [block[j * rows_all : (j + 1) * rows_all] for j in range(chunks)], axis=1
            )
        return jnp.dot(block, wgu[...], preferred_element_type=jnp.float32)

    loads[4].wait()
    loads[5].wait()
    for c in others:
        group_of(arrived, a_send, a_recv, c, lines).wait_recv()
        rs_out[c] = partial(c).astype(jnp.bfloat16)
        ctx_copy(rs_out.at[c], rs_in.at[my_c], p_send.at[c], p_recv.at[my_c], c).start()
    group_of(arrived, a_send, a_recv, my_c, lines - message).wait_recv()
    own[...] = partial(my_c)
    for load in loads[6:]:
        load.wait()
    for c in others:
        ctx_copy(k_hbm.at[0], kbuf.at[c], k_send.at[c], k_recv.at[c], c).wait_recv()
        ctx_copy(v_hbm.at[0], vbuf.at[c], v_send.at[c], v_recv.at[c], c).wait_recv()
    attend(0, mark)
    for c in others:
        ctx_copy(rs_out.at[c], rs_in.at[c], p_send.at[c], p_recv.at[c], c).wait_recv()
    sums = own[...]
    for c in others:
        sums = sums + rs_in[c].astype(jnp.float32)
    gate = sums[:, :units]
    hid[my_c] = (gate / (1.0 + jnp.exp(-gate)) * sums[:, units:]).astype(jnp.bfloat16)
    for c in others:
        ctx_copy(hid.at[my_c], hid.at[my_c], h_send.at[c], h_recv.at[my_c], c).start()

    def answer(c):
        block = jnp.dot(hid[c], wd_ref[...], preferred_element_type=jnp.float32).astype(
            jnp.bfloat16
        )
        if chunks > 1:
            block = jnp.concatenate(
                [block[:, j * wide : (j + 1) * wide] for j in range(chunks)], axis=0
            )
            block = jnp.dot(unsort[...], block, preferred_element_type=jnp.float32).astype(
                jnp.bfloat16
            )
        answers[c] = block

    answer(my_c)
    scatter(answers, ret, r_send, r_recv, my_c, 1)
    ret[my_c, my_rows] = answers[my_c, my_rows]
    for c in others:
        ctx_copy(hid.at[my_c], hid.at[c], h_send.at[c], h_recv.at[c], c).wait_recv()
        answer(c)
        scatter(answers, ret, r_send, r_recv, c, 0)
    attend(mark, heads)

    def combine(c):
        part = ret[c]
        mixed = jnp.dot(w_hi[...], part, preferred_element_type=jnp.float32) + jnp.dot(
            w_lo[...], part, preferred_element_type=jnp.float32
        )
        mixed = jnp.concatenate(
            [mixed[j * tokens : (j + 1) * tokens] for j in range(chunks)], axis=1
        )
        out_ref[0, :, pl.ds(pl.multiple_of(c * col, col), col)] = mixed.astype(jnp.bfloat16)

    group_of(ret, r_send, r_recv, my_c, lines - message).wait_recv()
    combine(my_c)
    for c in others:
        group_of(ret, r_send, r_recv, c, lines).wait_recv()
        combine(c)

    group_of(outgoing, a_send, a_recv, my_c, lines - message).wait_send()
    group_of(answers, r_send, r_recv, my_c, lines - message).wait_send()
    for c in others:
        ctx_copy(k_hbm.at[0], kbuf.at[c], k_send.at[c], k_recv.at[c], c).wait_send()
        ctx_copy(v_hbm.at[0], vbuf.at[c], v_send.at[c], v_recv.at[c], c).wait_send()
        group_of(outgoing, a_send, a_recv, c, lines).wait_send()
        ctx_copy(rs_out.at[c], rs_in.at[c], p_send.at[c], p_recv.at[c], c).wait_send()
        ctx_copy(hid.at[my_c], hid.at[c], h_send.at[c], h_recv.at[c], c).wait_send()
        group_of(answers, r_send, r_recv, c, lines).wait_send()


def shards(
    n_ctx, n_dp, queries, key_rows, value_rows, stream, norm_gain, expert_ids, gate_values,
    w_gate, w_up, w_down,
):
    tokens, width = stream.shape[1:]
    top = expert_ids.shape[2]
    kv = key_rows.shape[2]
    units = w_gate.shape[2]
    col = width // n_ctx
    slot, chunks = message_form(col)
    rows = n_dp * slot
    lines = rows * chunks
    wide = col // chunks
    order = lines if chunks > 1 else TILE
    bf16, f32 = jnp.bfloat16, jnp.float32
    scratch = [
        ((tokens, queries.shape[2]), bf16),
        ((tokens, width), bf16),
        ((1, width), f32),
        ((top, tokens), jnp.int32),
        ((top, tokens), f32),
        ((col, 2 * units), bf16),
        ((units, col), bf16),
        ((n_ctx, lines, wide), bf16),
        ((n_ctx, lines, wide), bf16),
        ((n_ctx, tokens, kv), bf16),
        ((n_ctx, tokens, kv), bf16),
        ((n_ctx, rows, 2 * units), bf16),
        ((n_ctx, rows, 2 * units), bf16),
        ((rows, 2 * units), f32),
        ((n_ctx, rows, units), bf16),
        ((n_ctx, lines, wide), bf16),
        ((n_ctx, lines, wide), bf16),
        ((chunks * tokens, lines), bf16),
        ((chunks * tokens, lines), bf16),
        ((order, order), bf16),
        ((order, order), bf16),
    ]
    need = sum(math.prod(s) * jnp.dtype(t).itemsize for s, t in scratch)
    hbm = pl.BlockSpec(memory_space=pltpu.HBM)
    vmem = pl.BlockSpec(memory_space=pltpu.VMEM)
    return pl.pallas_call(
        functools.partial(fused, n_ctx, n_dp, 6),
        out_shape=(
            jax.ShapeDtypeStruct(queries.shape, bf16),
            jax.ShapeDtypeStruct(stream.shape, bf16),
        ),
        in_specs=[hbm] * 10,
        out_specs=(vmem, vmem),
        scratch_shapes=[pltpu.VMEM(s, t) for s, t in scratch]
        + [pltpu.SemaphoreType.DMA((n_ctx,))] * 12
        + [pltpu.SemaphoreType.DMA((10,))],
        compiler_params=pltpu.CompilerParams(
            collective_id=0, has_side_effects=True, vmem_limit_bytes=need + (16 << 20)
        ),
    )(
        queries, key_rows, value_rows, stream, norm_gain.reshape(1, width),
        expert_ids.swapaxes(1, 2), gate_values.swapaxes(1, 2), w_gate, w_up, w_down,
    )


def solution(mesh):
    rows = P("dp", "ctx", None)
    return jax.shard_map(
        functools.partial(shards, mesh.shape["ctx"], mesh.shape["dp"]),
        mesh=mesh,
        in_specs=(rows,) * 4 + (P(),) + (rows,) * 4 + (P("dp", None, "ctx"),),
        out_specs=(rows, rows),
        check_vma=False,
    )
```

time: 59.1 us -> 53.4 us (0.904)
  Pallas kernels: 49.7 us -> 41.8 us
  local copies, waits for them, and re-layouts: 8.28 us -> 10.4 us
    pallas_call x1, Pallas kernels: 49.7 us -> 41.8 us  [shards(): pl.pallas_call(functools.partial(fused, n_ctx, n_dp, 6), out_shape=(jax.S...]
    unnamed x20 -> x22, local copies, waits for them, and re-layouts: 8.28 us -> 10.4 us
where the time goes in v2:
time: 53.4 us; the launch traced here: 52.8 us
  Pallas kernels  41.8 us (78%)
  local copies, waits for them, and re-layouts  10.4 us (19%)
  between operations  0.66 us (1%)
    pallas_call x1, Pallas kernels, shards(): pl.pallas_call(functools.partial(fused, n_ctx, n_dp, 6), out_shape=(jax.S...  41.8 us
    unnamed x22, local copies, waits for them, and re-layouts  10.4 us

profile of v2, /device:TPU:0, one launch (start us, length us, event | category | flops | bytes accessed | tf_op | source)
XLA Modules:
  0.0 52.8 jit_solution(13183163436705374376)
XLA Ops:
  0.6 0.0 copy-start.8
  0.6 0.7 %copy-done.8 = s32[1,128,8]{1,2,0:T(8,128)S(1)} copy-done((s32[1,128,8]{1,2,0:T(8,128)S(1)}, s32[1,128,8]{1,2,0:T(8,128)}, u32[]{:S(2)}) %copy-start.8) | copy-done | bytes 4120
  1.3 0.0 copy-start
  1.3 1.0 %copy-done = bf16[1,128,2048]{2,1,0:T(8,128)(2,1)S(1)} copy-done((bf16[1,128,2048]{2,1,0:T(8,128)(2,1)S(1)}, bf16[1,128,2048]{2,1,0:T(8,128)(2,1)}, u32[]{:S(2)}) %copy-start) | copy-done | bytes 524312
  2.4 0.0 copy-start.1
  2.4 1.0 %copy-done.1 = bf16[1,128,2048]{2,1,0:T(8,128)(2,1)S(1)} copy-done((bf16[1,128,2048]{2,1,0:T(8,128)(2,1)S(1)}, bf16[1,128,2048]{2,1,0:T(8,128)(2,1)}, u32[]{:S(2)}) %copy-start.1) | copy-done | bytes 524312
  3.4 0.0 copy-start.2
  3.4 1.0 %copy-done.2 = bf16[1,512,384]{2,1,0:T(8,128)(2,1)S(1)} copy-done((bf16[1,512,384]{2,1,0:T(8,128)(2,1)S(1)}, bf16[1,512,384]{2,1,0:T(8,128)(2,1)}, u32[]{:S(2)}) %copy-start.2) | copy-done | bytes 393240
  4.4 0.0 copy-start.3
  4.4 1.0 %copy-done.3 = bf16[1,512,384]{2,1,0:T(8,128)(2,1)S(1)} copy-done((bf16[1,512,384]{2,1,0:T(8,128)(2,1)S(1)}, bf16[1,512,384]{2,1,0:T(8,128)(2,1)}, u32[]{:S(2)}) %copy-start.3) | copy-done | bytes 393240
  5.4 0.0 copy-start.4
  5.4 1.0 %copy-done.4 = bf16[1,384,512]{2,1,0:T(8,128)(2,1)S(1)} copy-done((bf16[1,384,512]{2,1,0:T(8,128)(2,1)S(1)}, bf16[1,384,512]{2,1,0:T(8,128)(2,1)}, u32[]{:S(2)}) %copy-start.4) | copy-done | bytes 393240
  6.4 0.0 copy-start.5
  6.4 0.8 %copy-done.5 = bf16[1,128,256]{2,1,0:T(8,128)(2,1)S(1)} copy-done((bf16[1,128,256]{2,1,0:T(8,128)(2,1)S(1)}, bf16[1,128,256]{2,1,0:T(8,128)(2,1)}, u32[]{:S(2)}) %copy-start.5) | copy-done | bytes 65560
  7.2 0.0 copy-start.6
  7.2 0.8 %copy-done.6 = bf16[1,128,256]{2,1,0:T(8,128)(2,1)S(1)} copy-done((bf16[1,128,256]{2,1,0:T(8,128)(2,1)S(1)}, bf16[1,128,256]{2,1,0:T(8,128)(2,1)}, u32[]{:S(2)}) %copy-start.6) | copy-done | bytes 65560
  8.1 0.0 copy-start.7
  8.1 0.7 %copy-done.7 = f32[2048]{0:T(1024)S(1)} copy-done((f32[2048]{0:T(1024)S(1)}, f32[2048]{0:T(1024)}, u32[]{:S(2)}) %copy-start.7) | copy-done | bytes 8216
  8.8 0.0 copy-start.9
  8.8 0.7 %copy-done.9 = f32[1,128,8]{1,2,0:T(8,128)S(1)} copy-done((f32[1,128,8]{1,2,0:T(8,128)S(1)}, f32[1,128,8]{1,2,0:T(8,128)}, u32[]{:S(2)}) %copy-start.9) | copy-done | bytes 4120
  9.5 41.8 %shard_map.113 = (bf16[1,128,2048]{2,1,0:T(8,128)(2,1)S(1)}, bf16[1,128,2048]{2,1,0:T(8,128)(2,1)S(1)}) custom-call(bf16[1,128,2048]{2,1,0:T(8,128)(2,1)S(1)} %copy-done, bf16[1,128,256]{2,1,0:T(8,128)(2,1)S(1)} %copy-done.5, bf16[1,128,256]{2,1,0:T(8,128)(2,1)S(1)} %copy-done.6, bf16[1,128,2048]{2,1,0:T(8,128)(2,1)S(1)} %copy-done.1, ...), custom_call_target="tpu_custom_call" | custom-call | tf_op jit(solution)/shard_map/pallas_call | solution.py:328
  51.3 0.8 %copy.14 = bf16[1,128,2048]{2,1,0:T(8,128)(2,1)} copy(bf16[1,128,2048]{2,1,0:T(8,128)(2,1)S(1)} %get-tuple-element.4) | data formatting | bytes 1048576
  52.1 0.8 %copy.15 = bf16[1,128,2048]{2,1,0:T(8,128)(2,1)} copy(bf16[1,128,2048]{2,1,0:T(8,128)(2,1)S(1)} %get-tuple-element.5) | data formatting | bytes 1048576
Async XLA Ops:
  0.6 0.7 %copy-start.8 = (s32[1,128,8]{1,2,0:T(8,128)S(1)}, s32[1,128,8]{1,2,0:T(8,128)}, u32[]{:S(2)}) copy-start(s32[1,128,8]{1,2,0:T(8,128)} %param.15) | copy-start | bytes 12292
  1.3 1.0 %copy-start = (bf16[1,128,2048]{2,1,0:T(8,128)(2,1)S(1)}, bf16[1,128,2048]{2,1,0:T(8,128)(2,1)}, u32[]{:S(2)}) copy-start(bf16[1,128,2048]{2,1,0:T(8,128)(2,1)} %q_hbm.1) | copy-start | bytes 1572868
  2.4 1.0 %copy-start.1 = (bf16[1,128,2048]{2,1,0:T(8,128)(2,1)S(1)}, bf16[1,128,2048]{2,1,0:T(8,128)(2,1)}, u32[]{:S(2)}) copy-start(bf16[1,128,2048]{2,1,0:T(8,128)(2,1)} %s_hbm.1) | copy-start | bytes 1572868
  3.4 1.0 %copy-start.2 = (bf16[1,512,384]{2,1,0:T(8,128)(2,1)S(1)}, bf16[1,512,384]{2,1,0:T(8,128)(2,1)}, u32[]{:S(2)}) copy-start(bf16[1,512,384]{2,1,0:T(8,128)(2,1)} %wg_hbm.1) | copy-start | bytes 1179652
  4.4 1.0 %copy-start.3 = (bf16[1,512,384]{2,1,0:T(8,128)(2,1)S(1)}, bf16[1,512,384]{2,1,0:T(8,128)(2,1)}, u32[]{:S(2)}) copy-start(bf16[1,512,384]{2,1,0:T(8,128)(2,1)} %wu_hbm.1) | copy-start | bytes 1179652
  5.4 1.0 %copy-start.4 = (bf16[1,384,512]{2,1,0:T(8,128)(2,1)S(1)}, bf16[1,384,512]{2,1,0:T(8,128)(2,1)}, u32[]{:S(2)}) copy-start(bf16[1,384,512]{2,1,0:T(8,128)(2,1)} %wd_hbm.1) | copy-start | bytes 1179652
  6.4 0.8 %copy-start.5 = (bf16[1,128,256]{2,1,0:T(8,128)(2,1)S(1)}, bf16[1,128,256]{2,1,0:T(8,128)(2,1)}, u32[]{:S(2)}) copy-start(bf16[1,128,256]{2,1,0:T(8,128)(2,1)} %k_hbm.1) | copy-start | bytes 196612
  7.2 0.8 %copy-start.6 = (bf16[1,128,256]{2,1,0:T(8,128)(2,1)S(1)}, bf16[1,128,256]{2,1,0:T(8,128)(2,1)}, u32[]{:S(2)}) copy-start(bf16[1,128,256]{2,1,0:T(8,128)(2,1)} %v_hbm.1) | copy-start | bytes 196612
  8.1 0.7 %copy-start.7 = (f32[2048]{0:T(1024)S(1)}, f32[2048]{0:T(1024)}, u32[]{:S(2)}) copy-start(f32[2048]{0:T(1024)} %param.14) | copy-start | bytes 24580
  8.8 0.7 %copy-start.9 = (f32[1,128,8]{1,2,0:T(8,128)S(1)}, f32[1,128,8]{1,2,0:T(8,128)}, u32[]{:S(2)}) copy-start(f32[1,128,8]{1,2,0:T(8,128)} %param.16) | copy-start | bytes 12292
